TPU v7x, 32 devices: a whole 2x2x4 slice. The times are simulated.
32 devices in a mesh: mem: 8 (over z, core), lat: 2 (over y), lon: 2 (over x).
Axes of the slice: x: 2, y: 2, z: 4, core: 2. Of those that a mesh axis runs over, the one named last changes fastest.
Arguments:
- controls: float32 [16, 4, 64, 2048], P('mem', None, 'lat', 'lon'), may hold values from -6 to 6
- perturbations: float32 [16, 4, 64, 2048], P('mem', None, 'lat', 'lon'), may hold values from -3 to 3
- obs_mask: int32 [4, 64, 2048], P(None, 'lat', 'lon'), may hold values 0 or 1
- obs_weight: float32 [4, 64, 2048], P(None, 'lat', 'lon'), may hold values from 0.5 to 4
- lat_class: int32 [64], replicated, may hold values from 0 to 15
- lat_table: float32 [16, 15], replicated, may hold values from 0 to 0.25
- lon_table: float32 [16, 15], replicated, may hold values from 0 to 0.25
- lev_table: float32 [4, 15], replicated, may hold values from 0 to 1
Outputs:
- hess_product: float32 [16, 4, 64, 2048], P('mem', None, 'lat', 'lon')
All inputs are finite; a program needn't handle non-finite values. No bound on the sum of `obs_mask` on one device may be relied on, other than what follows from the above.
Results may differ from a plain program's by a relative error of at most 0.00005.
Values sent between devices are 32-bit elements; how exact they have to be, the bound alone decides.
A program may use at most 64 MiB of HBM per device.

v0:
```python
import jax
import jax.numpy as jnp
from jax import lax
from jax.sharding import PartitionSpec as P

TAPS = 15


PRECISE = lax.Precision.HIGHEST


def with_halo(block, sides, width, periodic):
    for axis, dim in sides:
        count = lax.axis_size(axis)
        forward = [(i, i + 1) for i in range(count - 1)]
        if periodic:
            forward.append((count - 1, 0))
        backward = [(target, source) for source, target in forward]
        low = lax.ppermute(
            lax.slice_in_dim(block, block.shape[dim] - width, None, axis=dim), axis, forward
        )
        high = lax.ppermute(lax.slice_in_dim(block, 0, width, axis=dim), axis, backward)
        block = jnp.concatenate([low, block, high], axis=dim)
    return block


def lookup(classes, table):
    levels = jnp.arange(table.shape[0], dtype=jnp.int32)
    onehot = (classes[:, None] == levels[None, :]).astype(jnp.float32)
    return jnp.dot(onehot, table, precision=PRECISE, preferred_element_type=jnp.float32)


def lat_forward(padded, coefs):
    row_count = coefs.shape[0]
    total = 0.0
    for tap_index in range(coefs.shape[1]):
        total = (
            total
            + coefs[:, tap_index][:, None] * padded[:, :, tap_index : tap_index + row_count, :]
        )
    return total


def lat_adjoint(padded, padded_coefs):
    margin = TAPS // 2
    row_count = padded.shape[2] - 2 * margin
    total = 0.0
    for tap_index in range(padded_coefs.shape[1]):
        lower = 2 * margin - tap_index
        total = (
            total
            + padded_coefs[lower : lower + row_count, tap_index][:, None]
            * padded[:, :, lower : lower + row_count, :]
        )
    return total


def lon_forward(padded, coefs):
    margin = TAPS // 2
    col_count = padded.shape[3] - 2 * margin
    total = 0.0
    for tap_index in range(coefs.shape[1]):
        total = (
            total + coefs[:, tap_index][:, None] * padded[..., tap_index : tap_index + col_count]
        )
    return total


def lon_adjoint(padded, coefs):
    margin = TAPS // 2
    col_count = padded.shape[3] - 2 * margin
    total = 0.0
    for tap_index in range(coefs.shape[1]):
        lower = 2 * margin - tap_index
        total = total + coefs[:, tap_index][:, None] * padded[..., lower : lower + col_count]
    return total


def lev_forward(field, coefs):
    margin = TAPS // 2
    level_count = field.shape[1]
    padded = jnp.pad(field, ((0, 0), (margin, margin), (0, 0), (0, 0)))
    total = 0.0
    for tap_index in range(coefs.shape[1]):
        total = (
            total
            + coefs[:, tap_index][:, None, None] * padded[:, tap_index : tap_index + level_count]
        )
    return total


def lev_adjoint(field, coefs):
    margin = TAPS // 2
    level_count = field.shape[1]
    padded = jnp.pad(field, ((0, 0), (margin, margin), (0, 0), (0, 0)))
    padded_coefs = jnp.pad(coefs, ((margin, margin), (0, 0)))
    total = 0.0
    for tap_index in range(coefs.shape[1]):
        lower = 2 * margin - tap_index
        total = (
            total
            + padded_coefs[lower : lower + level_count, tap_index][:, None, None]
            * padded[:, lower : lower + level_count]
        )
    return total


def per_device(
    controls, perturbations, obs_mask, obs_weight, lat_class, lat_table, lon_table, lev_table
):
    margin = TAPS // 2
    row_count = controls.shape[2]
    first_row = lax.axis_index("lat") * row_count
    class_padded = lax.dynamic_slice_in_dim(
        jnp.pad(lat_class, (margin, margin)), first_row, row_count + 2 * margin, 0
    )
    lat_padded_coefs = lookup(class_padded, lat_table)
    lon_padded_coefs = lookup(class_padded, lon_table)
    lat_coefs = lat_padded_coefs[margin : margin + row_count]
    lon_coefs = lon_padded_coefs[margin : margin + row_count]
    row_block = with_halo(controls, (("lat", 2),), margin, False)
    across = lat_forward(row_block, lat_coefs)
    col_block = with_halo(across, (("lon", 3),), margin, True)
    spread = lon_forward(col_block, lon_coefs)
    spread = lev_forward(spread, lev_table)
    partial_value = jnp.sum(perturbations * spread, axis=0)
    weighting = obs_weight * obs_mask.astype(jnp.float32)
    share_width = controls.shape[3] // lax.axis_size("mem")
    offset = lax.axis_index("mem") * share_width
    share = lax.psum_scatter(partial_value, "mem", scatter_dimension=2, tiled=True)
    weighted = lax.dynamic_slice_in_dim(weighting, offset, share_width, 2) * share
    weighted = lax.all_gather(weighted, "mem", axis=2, tiled=True)
    backed = lev_adjoint(perturbations * weighted[None], lev_table)
    col_block = with_halo(backed, (("lon", 3),), margin, True)
    along = lon_adjoint(col_block, lon_coefs)
    row_block = with_halo(along, (("lat", 2),), margin, False)
    result = lat_adjoint(row_block, lat_padded_coefs)
    return controls + result


def solution(mesh):
    return jax.shard_map(
        per_device,
        mesh=mesh,
        in_specs=(
            P("mem", None, "lat", "lon"),
            P("mem", None, "lat", "lon"),
            P(None, "lat", "lon"),
            P(None, "lat", "lon"),
            P(),
            P(),
            P(),
            P(),
        ),
        out_specs=P("mem", None, "lat", "lon"),
        check_vma=False,
    )
```

profile of v0, /device:TPU:0, one launch (start us, length us, event | category | flops | bytes accessed | tf_op | source)
XLA Modules:
  0.0 123.3 jit_solution(16091148031088721223)
XLA Ops:
  6.5 0.0 copy-start
  6.5 0.0 copy-start.1
  6.5 0.0 reduce-scatter.2.cloned.1.call-start
  6.5 1.2 fusion.193
  7.7 0.0 copy-start.3
  7.7 4.9 %collective-permute-start = (f32[2,4,7,1024]{3,2,1,0:T(8,128)S(1)}, f32[2,4,7,1024]{3,2,1,0:T(8,128)S(1)}, u32[]{:S(2)}, u32[]{:S(2)}) collective-permute-start(f32[2,4,7,1024]{3,2,1,0:T(8,128)S(1)} %get-tuple-element.30), channel_id=1, source_target_pairs={{0,2},{1,3},{4,6},{5,7},{8,10},{9,11},{12,14},{13,15},{16,18},{17,... | collective-permute-start | bytes 688136 | tf_op jit(solution)/shard_map/ppermute | solution.py:19
  12.6 1.3 %collective-permute-start.1 = (f32[2,4,7,1024]{3,2,1,0:T(8,128)S(1)}, f32[2,4,7,1024]{3,2,1,0:T(8,128)S(1)}, u32[]{:S(2)}, u32[]{:S(2)}) collective-permute-start(f32[2,4,7,1024]{3,2,1,0:T(8,128)S(1)} %get-tuple-element.29), channel_id=1, source_target_pairs={{2,0},{3,1},{6,4},{7,5},{10,8},{11,9},{14,12},{15,13},{18,16},{19,... | collective-permute-start | bytes 688136 | tf_op jit(solution)/shard_map/ppermute | solution.py:22
  13.9 0.7 pad_dynamic-slice_fusion
  14.7 0.0 copy-done
  14.7 0.2 fusion.181
  14.9 0.1 slice_bitcast_fusion.43
  15.0 0.1 slice_bitcast_fusion.41
  15.0 0.9 fusion.180
  15.9 0.1 slice_bitcast_fusion.42
  16.1 0.0 copy-done.1
  16.1 0.1 constant_dynamic-update-slice_fusion.1
  16.1 0.0 copy-done.3
  16.2 0.4 fusion.184
  16.6 5.7 %collective-permute-done.1 = f32[2,4,7,1024]{3,2,1,0:T(8,128)S(1)} collective-permute-done((f32[2,4,7,1024]{3,2,1,0:T(8,128)S(1)}, f32[2,4,7,1024]{3,2,1,0:T(8,128)S(1)}, u32[]{:S(2)}, u32[]{:S(2)}) %collective-permute-start.1) | collective-permute-done | bytes 229408 | tf_op jit(solution)/shard_map/ppermute | solution.py:22
  22.3 0.0 collective-permute-done
  22.3 2.2 %fusion.126 = f32[2,4,32,1024]{3,2,1,0:T(8,128)S(1)} fusion(f32[2,4,32,1024]{3,2,1,0:T(8,128)S(1)} %copy-done.1, f32[2,4,7,1024]{3,2,1,0:T(8,128)S(1)} %collective-permute-done, f32[2,4,39,1024]{3,2,1,0:T(8,128)S(1)} %constant_dynamic-update-slice_fusion, f32[32]{0:T(128)S(1)} %get-tuple-element.45, f32[32]{0:T(128)S(1)} %get-tuple-element.46, ...), kind=kLoop, calls=%fused_computation.222 | loop fusion | flops 9437184 | bytes 9668480 | tf_op jit(solution)/shard_map/add | solution.py:38
  24.6 0.1 fusion.192
  24.7 0.0 copy-start.2
  24.7 1.6 %collective-permute-start.3 = (f32[2,4,32,7]{3,2,1,0:T(8,128)S(1)}, f32[2,4,32,7]{3,2,1,0:T(8,128)S(1)}, u32[]{:S(2)}, u32[]{:S(2)}) collective-permute-start(f32[2,4,32,7]{3,2,1,0:T(8,128)S(1)} %get-tuple-element.28), channel_id=1, source_target_pairs={{1,0},{0,1},{3,2},{2,3},{5,4},{4,5},{7,6},{6,7},{9,8},{8,9},{11,10... | collective-permute-start | bytes 21512 | tf_op jit(solution)/shard_map/ppermute | solution.py:22
  26.2 0.5 collective-permute-start.2
  26.8 0.2 multiply_reduce_fusion.2
  27.0 3.2 %collective-permute-done.3 = f32[2,4,32,7]{3,2,1,0:T(8,128)S(1)} collective-permute-done((f32[2,4,32,7]{3,2,1,0:T(8,128)S(1)}, f32[2,4,32,7]{3,2,1,0:T(8,128)S(1)}, u32[]{:S(2)}, u32[]{:S(2)}) %collective-permute-start.3) | collective-permute-done | bytes 7200 | tf_op jit(solution)/shard_map/ppermute | solution.py:22
  30.2 1.4 %collective-permute-done.2 = f32[2,4,32,7]{3,2,1,0:T(8,128)S(1)} collective-permute-done((f32[2,4,32,7]{3,2,1,0:T(8,128)S(1)}, f32[2,4,32,7]{3,2,1,0:T(8,128)S(1)}, u32[]{:S(2)}, u32[]{:S(2)}) %collective-permute-start.2) | collective-permute-done | bytes 7200 | tf_op jit(solution)/shard_map/ppermute | solution.py:19
  31.6 5.3 %fusion.41 = f32[2,4,32,1024]{3,2,1,0:T(8,128)S(1)} fusion(f32[2,4,32,1024]{3,2,1,0:T(8,128)S(1)} %fusion.126, f32[2,4,32,7]{3,2,1,0:T(8,128)S(1)} %collective-permute-done.3, f32[2,4,32,7]{3,2,1,0:T(8,128)S(1)} %collective-permute-done.2, f32[32]{0:T(128)S(1)} %get-tuple-element.51, f32[32]{0:T(128)S(1)} %get-tuple-element.52, ...), kind=kLoop, calls=%fused_computation.137 | loop fusion | flops 11272192 | bytes 2113408 | tf_op jit(solution)/shard_map/add | solution.py:64
  36.9 0.0 copy-done.2
  36.9 1.5 %fusion.178 = f32[4,32,1024]{2,1,0:T(8,128)} fusion(f32[2,4,32,1024]{3,2,1,0:T(8,128)S(1)} %copy-done.2, f32[2,4,32,1024]{3,2,1,0:T(8,128)S(1)} %fusion.41, f32[4]{0:T(128)S(1)} %get-tuple-element.22, f32[4]{0:T(128)S(1)} %get-tuple-element.21, f32[4]{0:T(128)S(1)} %get-tuple-element.8, f32[4]{0:T(128)S(1)} %get-tuple-element.9, ...), kind=kLoop, calls=%fused_computation.288 | loop fusion | flops 5111808 | bytes 2621632 | tf_op jit(solution)/shard_map/reduce_sum | solution.py:126
  38.4 0.0 reduce-scatter.2.cloned.1.call-update
  38.4 31.3 %reduce-scatter.2.cloned.1.call-done = f32[4,32,128]{2,1,0:T(8,128)} async-done(((f32[4,32,1024]{2,1,0:T(8,128)}), f32[4,32,128]{2,1,0:T(8,128)}) %reduce-scatter.2.cloned.1.call-update) | async-done | bytes 65552 | tf_op jit(solution)/shard_map/reduce_scatter | solution.py:130
  69.7 0.9 fusion.179
  70.7 15.0 %all_gather.3 = f32[4,32,1024]{2,1,0:T(8,128)S(1)} all-gather(f32[4,32,128]{2,1,0:T(8,128)S(1)} %fusion.179), channel_id=1, replica_groups=mesh['mem'=8,'lat'=2,'lon'=2] {'mem'}, dimensions={2}, use_global_device_ids=true | all-gather | bytes 589824 | tf_op jit(solution)/shard_map/all_gather | solution.py:132
  85.7 0.1 broadcast_multiply_fusion
  85.8 0.4 fusion.165
  86.3 0.1 fusion.191
  86.4 1.6 %collective-permute-start.5 = (f32[2,4,32,7]{3,2,1,0:T(8,128)S(1)}, f32[2,4,32,7]{3,2,1,0:T(8,128)S(1)}, u32[]{:S(2)}, u32[]{:S(2)}) collective-permute-start(f32[2,4,32,7]{3,2,1,0:T(8,128)S(1)} %get-tuple-element.26), channel_id=1, source_target_pairs={{0,1},{1,0},{2,3},{3,2},{4,5},{5,4},{6,7},{7,6},{8,9},{9,8},{10,11... | collective-permute-start | bytes 21512 | tf_op jit(solution)/shard_map/ppermute | solution.py:19
  88.0 0.5 collective-permute-start.4
  88.5 4.3 %collective-permute-done.5 = f32[2,4,32,7]{3,2,1,0:T(8,128)S(1)} collective-permute-done((f32[2,4,32,7]{3,2,1,0:T(8,128)S(1)}, f32[2,4,32,7]{3,2,1,0:T(8,128)S(1)}, u32[]{:S(2)}, u32[]{:S(2)}) %collective-permute-start.5) | collective-permute-done | bytes 7200 | tf_op jit(solution)/shard_map/ppermute | solution.py:19
  92.7 2.2 %collective-permute-done.4 = f32[2,4,32,7]{3,2,1,0:T(8,128)S(1)} collective-permute-done((f32[2,4,32,7]{3,2,1,0:T(8,128)S(1)}, f32[2,4,32,7]{3,2,1,0:T(8,128)S(1)}, u32[]{:S(2)}, u32[]{:S(2)}) %collective-permute-start.4) | collective-permute-done | bytes 7200 | tf_op jit(solution)/shard_map/ppermute | solution.py:22
  95.0 5.3 %fusion.3 = f32[2,4,32,1024]{3,2,1,0:T(8,128)S(1)} fusion(f32[2,4,32,1024]{3,2,1,0:T(8,128)S(1)} %fusion.165, f32[2,4,32,7]{3,2,1,0:T(8,128)S(1)} %collective-permute-done.5, f32[2,4,32,7]{3,2,1,0:T(8,128)S(1)} %collective-permute-done.4, f32[32]{0:T(128)S(1)} %get-tuple-element.51, f32[32]{0:T(128)S(1)} %get-tuple-element.52, f32[32]{0:T(128)S(1)} %get-tuple-element.53, ...), kind=kLoop, calls=%fused_computation.99 | loop fusion | flops 11272192 | bytes 2113408 | tf_op jit(solution)/shard_map/add | solution.py:75
  100.3 3.4 %collective-permute-start.7 = (f32[2,4,7,1024]{3,2,1,0:T(8,128)S(1)}, f32[2,4,7,1024]{3,2,1,0:T(8,128)S(1)}, u32[]{:S(2)}, u32[]{:S(2)}) collective-permute-start(f32[2,4,7,1024]{3,2,1,0:T(8,128)S(1)} %get-tuple-element.24), channel_id=1, source_target_pairs={{0,2},{1,3},{4,6},{5,7},{8,10},{9,11},{12,14},{13,15},{16,18},{17,... | collective-permute-start | bytes 688136 | tf_op jit(solution)/shard_map/ppermute | solution.py:19
  103.8 1.3 %collective-permute-start.6 = (f32[2,4,7,1024]{3,2,1,0:T(8,128)S(1)}, f32[2,4,7,1024]{3,2,1,0:T(8,128)S(1)}, u32[]{:S(2)}, u32[]{:S(2)}) collective-permute-start(f32[2,4,7,1024]{3,2,1,0:T(8,128)S(1)} %get-tuple-element.23), channel_id=1, source_target_pairs={{2,0},{3,1},{6,4},{7,5},{10,8},{11,9},{14,12},{15,13},{18,16},{19,... | collective-permute-start | bytes 688136 | tf_op jit(solution)/shard_map/ppermute | solution.py:22
  105.1 3.9 %collective-permute-done.7 = f32[2,4,7,1024]{3,2,1,0:T(8,128)S(1)} collective-permute-done((f32[2,4,7,1024]{3,2,1,0:T(8,128)S(1)}, f32[2,4,7,1024]{3,2,1,0:T(8,128)S(1)}, u32[]{:S(2)}, u32[]{:S(2)}) %collective-permute-start.7) | collective-permute-done | bytes 229408 | tf_op jit(solution)/shard_map/ppermute | solution.py:19
  109.0 4.1 %collective-permute-done.6 = f32[2,4,7,1024]{3,2,1,0:T(8,128)S(1)} collective-permute-done((f32[2,4,7,1024]{3,2,1,0:T(8,128)S(1)}, f32[2,4,7,1024]{3,2,1,0:T(8,128)S(1)}, u32[]{:S(2)}, u32[]{:S(2)}) %collective-permute-start.6) | collective-permute-done | bytes 229408 | tf_op jit(solution)/shard_map/ppermute | solution.py:22
  113.1 3.4 %fusion.80 = f32[2,4,32,1024]{3,2,1,0:T(8,128)} fusion(f32[2,4,32,1024]{3,2,1,0:T(8,128)S(1)} %copy-done.1, f32[2,4,32,1024]{3,2,1,0:T(8,128)S(1)} %fusion.3, f32[2,4,7,1024]{3,2,1,0:T(8,128)S(1)} %collective-permute-done.7, f32[2,4,7,1024]{3,2,1,0:T(8,128)S(1)} %collective-permute-done.6, f32[32]{0:T(128)S(1)} %get-tuple-element.32, ...), kind=kLoop, calls=%fused_computation.176 | loop fusion | flops 11534336 | bytes 3606400 | tf_op jit(solution)/shard_map/add | solution.py:138
  (2 shorter events, 0.1 us)
Async XLA Ops:
  6.5 8.1 %copy-start = (f32[16,15]{1,0:T(8,128)S(1)}, f32[16,15]{1,0:T(8,128)}, u32[]{:S(2)}) copy-start(f32[16,15]{1,0:T(8,128)} %param.13) | copy-start | bytes 2884
  6.5 9.5 %copy-start.1 = (f32[2,4,32,1024]{3,2,1,0:T(8,128)S(1)}, f32[2,4,32,1024]{3,2,1,0:T(8,128)}, u32[]{:S(2)}) copy-start(f32[2,4,32,1024]{3,2,1,0:T(8,128)} %param.8) | copy-start | bytes 3145732
  6.5 63.2 %reduce-scatter.2.cloned.1.call-start = ((), (), s32[]{:S(2)}) async-start(), calls=%async_computation.1 | async-start | bytes 589824 | tf_op jit(solution)/shard_map/reduce_scatter | solution.py:130
  7.7 8.4 %copy-start.3 = (f32[4,15]{1,0:T(4,128)S(1)}, f32[4,15]{1,0:T(4,128)}, u32[]{:S(2)}) copy-start(f32[4,15]{1,0:T(4,128)} %param.15) | copy-start | bytes 724
  7.7 14.6 %collective-permute-start = (f32[2,4,7,1024]{3,2,1,0:T(8,128)S(1)}, f32[2,4,7,1024]{3,2,1,0:T(8,128)S(1)}, u32[]{:S(2)}, u32[]{:S(2)}) collective-permute-start(f32[2,4,7,1024]{3,2,1,0:T(8,128)S(1)} %get-tuple-element.30), channel_id=1, source_target_pairs={{0,2},{1,3},{4,6},{5,7},{8,10},{9,11},{12,14},{13,15},{16,18},{17,... | collective-permute-start | bytes 688136 | tf_op jit(solution)/shard_map/ppermute | solution.py:19
  12.6 9.7 %collective-permute-start.1 = (f32[2,4,7,1024]{3,2,1,0:T(8,128)S(1)}, f32[2,4,7,1024]{3,2,1,0:T(8,128)S(1)}, u32[]{:S(2)}, u32[]{:S(2)}) collective-permute-start(f32[2,4,7,1024]{3,2,1,0:T(8,128)S(1)} %get-tuple-element.29), channel_id=1, source_target_pairs={{2,0},{3,1},{6,4},{7,5},{10,8},{11,9},{14,12},{15,13},{18,16},{19,... | collective-permute-start | bytes 688136 | tf_op jit(solution)/shard_map/ppermute | solution.py:22
  24.7 12.2 %copy-start.2 = (f32[2,4,32,1024]{3,2,1,0:T(8,128)S(1)}, f32[2,4,32,1024]{3,2,1,0:T(8,128)}, u32[]{:S(2)}) copy-start(f32[2,4,32,1024]{3,2,1,0:T(8,128)} %param.9) | copy-start | bytes 3145732
  24.7 5.5 %collective-permute-start.3 = (f32[2,4,32,7]{3,2,1,0:T(8,128)S(1)}, f32[2,4,32,7]{3,2,1,0:T(8,128)S(1)}, u32[]{:S(2)}, u32[]{:S(2)}) collective-permute-start(f32[2,4,32,7]{3,2,1,0:T(8,128)S(1)} %get-tuple-element.28), channel_id=1, source_target_pairs={{1,0},{0,1},{3,2},{2,3},{5,4},{4,5},{7,6},{6,7},{9,8},{8,9},{11,10... | collective-permute-start | bytes 21512 | tf_op jit(solution)/shard_map/ppermute | solution.py:22
  26.2 5.4 %collective-permute-start.2 = (f32[2,4,32,7]{3,2,1,0:T(8,128)S(1)}, f32[2,4,32,7]{3,2,1,0:T(8,128)S(1)}, u32[]{:S(2)}, u32[]{:S(2)}) collective-permute-start(f32[2,4,32,7]{3,2,1,0:T(8,128)S(1)} %get-tuple-element.27), channel_id=1, source_target_pairs={{0,1},{1,0},{2,3},{3,2},{4,5},{5,4},{6,7},{7,6},{8,9},{9,8},{10,11... | collective-permute-start | bytes 21512 | tf_op jit(solution)/shard_map/ppermute | solution.py:19
  86.4 6.4 %collective-permute-start.5 = (f32[2,4,32,7]{3,2,1,0:T(8,128)S(1)}, f32[2,4,32,7]{3,2,1,0:T(8,128)S(1)}, u32[]{:S(2)}, u32[]{:S(2)}) collective-permute-start(f32[2,4,32,7]{3,2,1,0:T(8,128)S(1)} %get-tuple-element.26), channel_id=1, source_target_pairs={{0,1},{1,0},{2,3},{3,2},{4,5},{5,4},{6,7},{7,6},{8,9},{9,8},{10,11... | collective-permute-start | bytes 21512 | tf_op jit(solution)/shard_map/ppermute | solution.py:19
  88.0 7.0 %collective-permute-start.4 = (f32[2,4,32,7]{3,2,1,0:T(8,128)S(1)}, f32[2,4,32,7]{3,2,1,0:T(8,128)S(1)}, u32[]{:S(2)}, u32[]{:S(2)}) collective-permute-start(f32[2,4,32,7]{3,2,1,0:T(8,128)S(1)} %get-tuple-element.25), channel_id=1, source_target_pairs={{1,0},{0,1},{3,2},{2,3},{5,4},{4,5},{7,6},{6,7},{9,8},{8,9},{11,10... | collective-permute-start | bytes 21512 | tf_op jit(solution)/shard_map/ppermute | solution.py:22
  100.3 8.7 %collective-permute-start.7 = (f32[2,4,7,1024]{3,2,1,0:T(8,128)S(1)}, f32[2,4,7,1024]{3,2,1,0:T(8,128)S(1)}, u32[]{:S(2)}, u32[]{:S(2)}) collective-permute-start(f32[2,4,7,1024]{3,2,1,0:T(8,128)S(1)} %get-tuple-element.24), channel_id=1, source_target_pairs={{0,2},{1,3},{4,6},{5,7},{8,10},{9,11},{12,14},{13,15},{16,18},{17,... | collective-permute-start | bytes 688136 | tf_op jit(solution)/shard_map/ppermute | solution.py:19
  103.8 9.4 %collective-permute-start.6 = (f32[2,4,7,1024]{3,2,1,0:T(8,128)S(1)}, f32[2,4,7,1024]{3,2,1,0:T(8,128)S(1)}, u32[]{:S(2)}, u32[]{:S(2)}) collective-permute-start(f32[2,4,7,1024]{3,2,1,0:T(8,128)S(1)} %get-tuple-element.23), channel_id=1, source_target_pairs={{2,0},{3,1},{6,4},{7,5},{10,8},{11,9},{14,12},{15,13},{18,16},{19,... | collective-permute-start | bytes 688136 | tf_op jit(solution)/shard_map/ppermute | solution.py:22
Sparse Core Ops, SparseCore 0:
  38.5 31.1 reduce-scatter.1
where the time goes:
time: 124 us; the launch traced here: 123 us
  waiting for transfers between devices  56.2 us (45%)
  other arithmetic  19.8 us (16%)
  starting transfers between devices  15.1 us (12%)
  blocking collectives  15 us (12%)
  between operations  13.6 us (11%)
  local copies, waits for them, and re-layouts  2.53 us (2%)
    reduce_scatter x1, waiting for transfers between devices, per_device(): lax.psum_scatter(partial_value, 'mem', scatter_dimension=2, tiled=True)  31.3 us
    ppermute x4, waiting for transfers between devices, with_halo(): lax.ppermute(lax.slice_in_dim(block, 0, width, axis=dim), axis, backward)  15.3 us
    all_gather x1, blocking collectives, per_device(): weighted = lax.all_gather(weighted, 'mem', axis=2, tiled=True)  15 us
    ppermute x4, starting transfers between devices, with_halo(): lax.ppermute(lax.slice_in_dim(block, block.shape[dim] - width, None, axis...  10.5 us
    ppermute x4, waiting for transfers between devices, with_halo(): lax.ppermute(lax.slice_in_dim(block, block.shape[dim] - width, None, axis...  9.63 us
    add x1, other arithmetic, lon_adjoint(): total + coefs[:, tap_index][:, None] * padded[..., lower:lower + col_count]  5.29 us
    add x1, other arithmetic, lon_forward(): total + coefs[:, tap_index][:, None] * padded[..., tap_index:tap_index +...  5.28 us
    ppermute x4, starting transfers between devices, with_halo(): lax.ppermute(lax.slice_in_dim(block, 0, width, axis=dim), axis, backward)  4.62 us
  transfers between devices with their start and end apart: 9, of which 8 were waited for; matrix products, arithmetic and copies ran while one was open for 2% of the time, Pallas kernels for 0%

commit v1 on v0

v1 whole, which is shorter than its diff:
```python
import functools

import jax
import jax.numpy as jnp
from jax import lax
from jax.experimental import pallas as pl
from jax.experimental.pallas import tpu as pltpu
from jax.sharding import PartitionSpec as P

LANES = 128
SUB = 8


def by_offset(coefs, offset):
    taps = jnp.arange(coefs.shape[-1], dtype=jnp.int32)
    hit = offset[..., None] == taps
    return jnp.sum(jnp.where(hit, coefs, 0.0), axis=-1)


def lookup(classes, valid, table):
    rows = jnp.arange(table.shape[0], dtype=jnp.int32)
    hit = (classes[:, None] == rows[None, :]) & valid[:, None]
    return jnp.sum(jnp.where(hit[:, :, None], table[None], 0.0), axis=1)


def matrices(lat_class, lat_table, lon_table, lev_table, rows, levels):
    taps = lat_table.shape[1]
    h = taps // 2
    ext = rows + 2 * SUB
    first = lax.axis_index("lat") * rows
    classes = lax.dynamic_slice_in_dim(jnp.pad(lat_class, (SUB, SUB)), first, ext, 0)
    where = first - SUB + jnp.arange(ext, dtype=jnp.int32)
    valid = (where >= 0) & (where < lat_class.shape[0])
    lat_ext = lookup(classes, valid, lat_table)
    lon_ext = lookup(classes, valid, lon_table)
    i = jnp.arange(rows, dtype=jnp.int32)[:, None]
    e = jnp.arange(ext, dtype=jnp.int32)[None, :]
    ahead = by_offset(lat_ext[SUB : SUB + rows][:, None, :], e - SUB - i + h)
    ahead = jnp.where(valid[None, :], ahead, 0.0)
    back = by_offset(lat_ext[None, :, :], i - (e - SUB) + h)
    l = jnp.arange(levels, dtype=jnp.int32)
    mix = by_offset(lev_table[:, None, :], l[None, :] - l[:, None] + h)
    g = mix[:, None, :, None] * ahead[None, :, None, :]
    gt = mix.T[:, None, :, None] * back[None, :, None, :]
    both = jnp.stack([g, gt]).reshape(2, levels * rows, levels * ext)
    return both, lon_ext


def split(x):
    hi = x.astype(jnp.bfloat16)
    return hi, (x - hi.astype(jnp.float32)).astype(jnp.bfloat16)


def kernel(
    dims, ctrl, pert, mask, wgt, g_ref, lonc, out,
    X, Q, Wt, Mk, S, SR, CR, U, Y, D, V, F, R1, R2, WH, B, GS,
    loc, ysend, yrecv, xsend, xrecv, csend, crecv, s1, r1, s2, r2, s3, r3, s4, r4, s5, r5,
):
    n_mem, n_lat, n_lon, members, levels, rows, cols, taps, nt = dims
    h = taps // 2
    nb = cols // LANES + 1
    width = nb * LANES
    rt_n = rows // SUB
    ext = rows + 2 * SUB
    chips = n_mem // 2
    half = nt // 2
    shard = half // chips
    edge = levels * nb
    mem, lat, lon = lax.axis_index("mem"), lax.axis_index("lat"), lax.axis_index("lon")
    z, c = mem // 2, lax.rem(mem, 2)
    sib = mem + 1 - 2 * c
    lon_to = [lax.rem(lon + 1, n_lon)] + ([lax.rem(lon + n_lon - 1, n_lon)] if n_lon > 2 else [])
    lat_to = ((lat - 1, lat > 0, 1), (lat + 1, lat < n_lat - 1, 0))

    main = pl.ds(SUB, rows)
    loads = [
        pltpu.make_async_copy(ctrl, X.at[:, :, main, pl.ds(0, cols)], loc.at[0]),
        pltpu.make_async_copy(pert, Q.at[:, :, main, pl.ds(0, cols)], loc.at[1]),
        pltpu.make_async_copy(wgt, Wt, loc.at[2]),
        pltpu.make_async_copy(mask, Mk, loc.at[3]),
    ]
    for load in loads:
        load.start()

    barrier = pltpu.get_barrier_semaphore()

    def greet(**where):
        pl.semaphore_signal(barrier, inc=1, device_id=where, device_id_type=pl.DeviceIdType.MESH)

    greet(mem=sib)
    for k in range(1, chips):
        greet(mem=lax.rem(z + k, chips) * 2 + c)
    for x in lon_to:
        greet(lon=x)
    for there, exists, _ in lat_to:
        @pl.when(exists)
        def _():
            greet(lat=there)
            for x in lon_to:
                greet(lat=there, lon=x)
    peers = chips + len(lon_to)
    for _, exists, _ in lat_to:
        peers += jnp.where(exists, 1 + len(lon_to), 0)
    pl.semaphore_wait(barrier, peers)

    def remote(src, dst, send, recv, **where):
        return pltpu.make_async_remote_copy(
            src_ref=src, dst_ref=dst, send_sem=send, recv_sem=recv,
            device_id=where, device_id_type=pl.DeviceIdType.MESH,
        )

    def row_copies(side, there):
        mine = pl.ds(0 if side else rows - SUB, SUB)
        its = pl.ds(rows + SUB if side else 0, SUB)
        return [
            remote(src.at[:, :, mine], dst.at[:, :, its, pl.ds(0, cols)], ysend.at[side, a], yrecv.at[side, a], lat=there)
            for a, (src, dst) in enumerate(((ctrl, X), (pert, Q)))
        ]

    for there, exists, side in lat_to:
        @pl.when(exists)
        def _():
            for copy in row_copies(side, there):
                copy.start()

    for t in range(taps):
        B[t] = jnp.broadcast_to(lonc[:, t : t + 1], (ext, LANES))
    n_rows = levels * rows
    for a in range(2):
        hi, lo = split(g_ref[a])
        GS[a, 0:n_rows] = hi
        GS[a, n_rows : 2 * n_rows] = lo

    lane = lax.broadcasted_iota(jnp.int32, (SUB, LANES), 1)
    windows = [(16, 32 * m) for m in range(members)]
    centre = 32 * members - 8
    windows += [(8, centre + 16 * m) for m in range(members)] + [(8, centre + 16 * members)]
    assert centre + 16 * members + 24 <= LANES

    for load in loads:
        load.wait()

    def pack(idx, carry):
        l, r = idx // rt_n, pl.multiple_of(lax.rem(idx, rt_n) * SUB, SUB)
        total = jnp.zeros((SUB, LANES), jnp.float32)
        here, inner = pl.ds(r, SUB), pl.ds(r + SUB, SUB)
        first, last = pl.ds(0, LANES), pl.ds(cols - LANES, LANES)
        wm = [Wt[l, here, at] * Mk[l, here, at].astype(jnp.float32) for at in (first, last)]
        ends = [(X[m, l, inner, first], X[m, l, inner, last]) for m in range(members)]
        ends += [(Q[m, l, inner, first], Q[m, l, inner, last]) for m in range(members)]
        ends += [tuple(wm)]
        for (reach, at), (low, high) in zip(windows, ends):
            part = jnp.where(lane < reach, low, jnp.where(lane >= LANES - reach, high, 0.0))
            total += pltpu.roll(part, at, 1) if at else part
        S[l, here] = total
        return carry

    lax.fori_loop(0, levels * rt_n, pack, 0)

    strips = [remote(S, SR.at[a], xsend.at[a], xrecv.at[a], lon=x) for a, x in enumerate(lon_to)]
    for copy in strips:
        copy.start()

    def corner_copies(side, there):
        mine = pl.ds(0 if side else rows - SUB, SUB)
        return [
            remote(S.at[:, mine], CR.at[side, a], csend.at[side, a], crecv.at[side, a], lat=there, lon=x)
            for a, x in enumerate(lon_to)
        ]

    for there, exists, side in lat_to:
        @pl.when(exists)
        def _():
            for copy in corner_copies(side, there):
                copy.start()

    for side, there, exists in ((0, lat - 1, lat > 0), (1, lat + 1, lat < n_lat - 1)):
        its = pl.ds(rows + SUB if side else 0, SUB)

        @pl.when(jnp.logical_not(exists))
        def _():
            for m in range(members):
                for l in range(levels):
                    X[m, l, its] = jnp.zeros((SUB, width), jnp.float32)
                    Y[m, l, its] = jnp.zeros((SUB, cols), jnp.float32)

    def weigh(idx, carry):
        rt, l = idx // levels, lax.rem(idx, levels)
        r = pl.ds(pl.multiple_of(rt * SUB, SUB), SUB)
        for b in range(nb - 1):
            at = pl.ds(b * LANES, LANES)
            V[idx * nb + b] = Wt[l, r, at] * Mk[l, r, at].astype(jnp.float32)
        return carry

    lax.fori_loop(0, levels * rt_n, weigh, 0)

    def unpack(w, read):
        at = windows[w][1]
        got = read(0) if n_lon == 2 else None
        if got is None:
            a, b = read(1), read(0)
            a = pltpu.roll(a, LANES - at, 1) if at else a
            b = pltpu.roll(b, LANES - at, 1) if at else b
            return jnp.where(lane < LANES // 2, a, b)
        return pltpu.roll(got, LANES - at, 1) if at else got

    for copy in strips:
        copy.wait()
    strip = pl.ds(cols, LANES)

    def spread_strip(idx, carry):
        rt, l = idx // levels, lax.rem(idx, levels)
        r = pl.multiple_of(rt * SUB, SUB)
        for w in range(2 * members + 1):
            value = unpack(w, lambda a: SR[a, l, pl.ds(r, SUB)])
            if w < members:
                X[w, l, pl.ds(r + SUB, SUB), strip] = value
            elif w < 2 * members:
                Q[w - members, l, pl.ds(r + SUB, SUB), strip] = value
            else:
                V[idx * nb + nb - 1] = value
        return carry

    lax.fori_loop(0, levels * rt_n, spread_strip, 0)

    for there, exists, side in lat_to:
        @pl.when(exists)
        def _():
            row_copies(side, there)[0].wait_send()
            for copy in corner_copies(side, there):
                copy.wait_send()
    for side, there, exists in ((0, lat - 1, lat > 0), (1, lat + 1, lat < n_lat - 1)):
        its = pl.ds(rows + SUB if side else 0, SUB)

        @pl.when(exists)
        def _():
            row_copies(side, there)[0].wait_recv()
            for copy in corner_copies(side, there):
                copy.wait_recv()
            for l in range(levels):
                for w in range(2 * members):
                    value = unpack(w, lambda a: CR[side, a, l])
                    if w < members:
                        X[w, l, its, strip] = value
                    else:
                        Q[w - members, l, its, strip] = value

    def product(a, x):
        hi, lo = split(x)
        f32 = jnp.float32
        both = jnp.dot(GS[a], hi, preferred_element_type=f32)
        return both[:n_rows] + both[n_rows:] + jnp.dot(GS[a, 0:n_rows], lo, preferred_element_type=f32)

    for m in range(members):
        for lo_col in range(0, width, 2 * LANES):
            w = min(2 * LANES, width - lo_col)
            x = X[m, :, :, lo_col : lo_col + w].reshape(levels * ext, w)
            U[m, :, :, lo_col : lo_col + w] = product(0, x).reshape(levels, rows, w)

    def along(u, tile, forward):
        total = None
        for t in range(taps):
            s = (h - t) if forward else (t - h)
            moved = pltpu.roll(u, s % width, 1) if s else u
            coef = B[t, pl.ds(pl.multiple_of(tile * SUB, SUB), SUB)]
            term = jnp.concatenate([coef] * nb, axis=1) * moved
            total = term if total is None else total + term
        return total

    def forward(idx, carry):
        rt, l = idx // levels, lax.rem(idx, levels)
        r = pl.multiple_of(rt * SUB, SUB)
        total = None
        for m in range(members):
            term = Q[m, l, pl.ds(r + SUB, SUB)] * along(U[m, l, pl.ds(r, SUB)], rt + 1, True)
            total = term if total is None else total + term
        for b in range(nb):
            D[idx * nb + b] = total[:, b * LANES : (b + 1) * LANES]
        return carry

    lax.fori_loop(0, levels * rt_n, forward, 0)
    for i in range(rt_n * edge, nt):
        D[i] = jnp.zeros((SUB, LANES), jnp.float32)
        V[i] = jnp.zeros((SUB, LANES), jnp.float32)

    base = c * half
    pair = remote(D.at[pl.ds((1 - c) * half, half)], R1, s1, r1, mem=sib)
    pair.start()
    pair.wait_recv()
    to_owner = []
    for k in range(1, chips):
        tz = lax.rem(z + k, chips)
        at = tz * shard

        def add(i, carry, at=at):
            D[base + at + i] += R1[at + i]
            return carry

        lax.fori_loop(0, shard, add, 0)
        copy = remote(D.at[pl.ds(base + at, shard)], R2.at[k - 1], s2.at[k - 1], r2.at[k - 1], mem=tz * 2 + c)
        copy.start()
        to_owner.append(copy)
    for copy in to_owner:
        copy.wait_recv()

    own = z * shard

    def finish(i, carry):
        total = D[base + own + i] + R1[own + i]
        for k in range(1, chips):
            total += R2[k - 1, i]
        F[base + own + i] = total * V[base + own + i]
        return carry

    lax.fori_loop(0, shard, finish, 0)

    mine = F.at[pl.ds(base + own, shard)]
    back = [
        remote(mine, mine, s3.at[k - 1], r3.at[k - 1], mem=lax.rem(z + k, chips) * 2 + c)
        for k in range(1, chips)
    ]
    passed = [remote(mine, mine, s4.at[0], r4.at[0], mem=sib)]
    for copy in back + passed:
        copy.start()
    for k in range(1, chips):
        back[k - 1].wait_recv()
        got = F.at[pl.ds(base + lax.rem(z - k + chips, chips) * shard, shard)]
        copy = remote(got, got, s4.at[k], r4.at[k], mem=sib)
        copy.start()
        passed.append(copy)
    for copy in passed:
        copy.wait_recv()

    def edge_copy(side, there):
        at = 0 if side else (rt_n - 1) * edge
        return remote(F.at[pl.ds(at, edge)], WH.at[side], s5.at[side], r5.at[side], lat=there)

    for there, exists, side in lat_to:
        @pl.when(exists)
        def _():
            edge_copy(side, there).start()

    def backward_tile(l, r, tile, read):
        w = jnp.concatenate([read(b) for b in range(nb)], axis=1)
        for m in range(members):
            Y[m, l, pl.ds(r, SUB)] = along(Q[m, l, pl.ds(r, SUB)] * w, tile, False)[:, :cols]

    def backward(idx, carry):
        rt, l = idx // levels, lax.rem(idx, levels)
        r = pl.multiple_of(rt * SUB + SUB, SUB)
        backward_tile(l, r, rt + 1, lambda b: F[idx * nb + b])
        return carry

    lax.fori_loop(0, levels * rt_n, backward, 0)

    for side, there, exists in ((0, lat - 1, lat > 0), (1, lat + 1, lat < n_lat - 1)):
        tile = rt_n + 1 if side else 0

        @pl.when(exists)
        def _():
            row_copies(side, there)[1].wait_recv()
            edge_copy(side, there).wait_recv()

            def halo(l, carry):
                backward_tile(l, tile * SUB, tile, lambda b: WH[side, l * nb + b])
                return carry

            lax.fori_loop(0, levels, halo, 0)

    for m in range(members):
        for lo_col in range(0, cols, 2 * LANES):
            at = slice(lo_col, lo_col + 2 * LANES)
            y = Y[m, :, :, at].reshape(levels * ext, 2 * LANES)
            out[m, :, :, at] = X[m, :, SUB : SUB + rows, at] + product(1, y).reshape(levels, rows, 2 * LANES)

    pair.wait_send()
    for copy in to_owner + back + passed:
        copy.wait_send()
    for there, exists, side in lat_to:
        @pl.when(exists)
        def _():
            row_copies(side, there)[1].wait_send()
            edge_copy(side, there).wait_send()


def solution(mesh):
    n_mem, n_lat, n_lon = mesh.shape["mem"], mesh.shape["lat"], mesh.shape["lon"]

    def per_device(controls, perturbations, obs_mask, obs_weight, lat_class, lat_table, lon_table, lev_table):
        members, levels, rows, cols = controls.shape
        taps = lat_table.shape[1]
        nb = cols // LANES + 1
        width, ext, rt_n = nb * LANES, rows + 2 * SUB, rows // SUB
        nt = -(-(levels * rt_n * nb) // n_mem) * n_mem
        chips = n_mem // 2
        shard = nt // n_mem
        both, lon_ext = matrices(lat_class, lat_table, lon_table, lev_table, rows, levels)
        dims = (n_mem, n_lat, n_lon, members, levels, rows, cols, taps, nt)
        f32 = jnp.float32
        dma = pltpu.SemaphoreType.DMA
        sides = 1 if n_lon == 2 else 2
        hbm, vmem = pl.BlockSpec(memory_space=pl.ANY), pl.BlockSpec(memory_space=pltpu.VMEM)
        tiles = lambda *n: pltpu.VMEM((*n, SUB, LANES), f32)
        return pl.pallas_call(
            functools.partial(kernel, dims),
            out_shape=jax.ShapeDtypeStruct(controls.shape, f32),
            in_specs=[hbm] * 4 + [vmem] * 2,
            out_specs=vmem,
            scratch_shapes=[
                pltpu.VMEM((members, levels, ext, width), f32),
                pltpu.VMEM((members, levels, ext, width), f32),
                pltpu.VMEM((levels, rows, cols), f32),
                pltpu.VMEM((levels, rows, cols), jnp.int32),
                pltpu.VMEM((levels, rows, LANES), f32),
                pltpu.VMEM((sides, levels, rows, LANES), f32),
                pltpu.VMEM((2, sides, levels, SUB, LANES), f32),
                pltpu.VMEM((members, levels, rows, width), f32),
                pltpu.VMEM((members, levels, ext, cols), f32),
                tiles(nt), tiles(nt), tiles(nt),
                tiles(nt // 2), tiles(max(chips - 1, 1), shard), tiles(2, levels * nb),
                pltpu.VMEM((taps, ext, LANES), f32),
                pltpu.VMEM((2, 2 * levels * rows, levels * ext), jnp.bfloat16),
                dma((4,)), dma((2, 2)), dma((2, 2)), dma((sides,)), dma((sides,)), dma((2, sides)), dma((2, sides)),
                dma(()), dma(()), dma((chips,)), dma((chips,)), dma((chips,)), dma((chips,)),
                dma((chips,)), dma((chips,)), dma((2,)), dma((2,)),
            ],
            compiler_params=pltpu.CompilerParams(
                collective_id=0, has_side_effects=True, vmem_limit_bytes=48 * 1024 * 1024
            ),
        )(controls, perturbations, obs_mask, obs_weight, both, lon_ext)

    return jax.shard_map(
        per_device,
        mesh=mesh,
        in_specs=(
            P("mem", None, "lat", "lon"),
            P("mem", None, "lat", "lon"),
            P(None, "lat", "lon"),
            P(None, "lat", "lon"),
            P(),
            P(),
            P(),
            P(),
        ),
        out_specs=P("mem", None, "lat", "lon"),
        check_vma=False,
    )
```

time: 124 us -> 51.4 us (0.41)
  waiting for transfers between devices: 56.2 us -> 0 us
  Pallas kernels: 0 us -> 44 us
  other arithmetic: 19.8 us -> 0.7 us
  starting transfers between devices: 15.1 us -> 0 us
  blocking collectives: 15 us -> 0 us
  between operations: 13.6 us -> 0.09 us
  local copies, waits for them, and re-layouts: 2.53 us -> 6.32 us
    pallas_call x0 -> x1, Pallas kernels: none -> 44 us  [per_device(): pl.pallas_call(functools.partial(kernel, dims), out_shape=jax.ShapeDtypeS...]
    reduce_scatter x1 -> x0, waiting for transfers between devices: 31.3 us -> none  [per_device(): lax.psum_scatter(partial_value, 'mem', scatter_dimension=2, tiled=True)]
    ppermute x8 -> x0, waiting for transfers between devices: 24.9 us -> none  [the longest x4 15.3 us: with_halo(): lax.ppermute(lax.slice_in_dim(block, 0, width, axis=dim), axis, backward)]
    add x5 -> x2, other arithmetic: 16.6 us -> 0.01 us  [the longest x1 0.01 us: matrices(): ahead = by_offset(lat_ext[SUB:SUB + rows][:, None, :], e - SUB - i + h)]
    ppermute x8 -> x0, starting transfers between devices: 15.1 us -> none  [the longest x4 10.5 us: with_halo(): lax.ppermute(lax.slice_in_dim(block, block.shape[dim] - width, None, axis...]
    all_gather x1 -> x0, blocking collectives: 15 us -> none  [per_device(): weighted = lax.all_gather(weighted, 'mem', axis=2, tiled=True)]
    unnamed x9 -> x19, local copies, waits for them, and re-layouts: 0.09 us -> 5.66 us
    slice x4 -> x1, local copies, waits for them, and re-layouts: 1.39 us -> 0.07 us  [matrices(): ahead = by_offset(lat_ext[SUB:SUB + rows][:, None, :], e - SUB - i + h)]
  transfers between devices with their start and end apart: 9 -> 0, of which waited for: 8 -> 0; matrix products, arithmetic and copies ran while one was open for 2% -> 0% of each run, Pallas kernels for 0% -> 0%
where the time goes in v1:
time: 51.4 us; the launch traced here: 51.1 us
  Pallas kernels  44 us (86%)
  local copies, waits for them, and re-layouts  6.32 us (12%)
  other arithmetic  0.7 us (1%)
    pallas_call x1, Pallas kernels, per_device(): pl.pallas_call(functools.partial(kernel, dims), out_shape=jax.ShapeDtypeS...  44 us
    unnamed x19, local copies, waits for them, and re-layouts  5.66 us

profile of v1, /device:TPU:0, one launch (start us, length us, event | category | flops | bytes accessed | tf_op | source)
XLA Modules:
  0.0 51.1 jit_solution(6134998958340474370)
XLA Ops:
  0.0 0.0 copy-start.7
  0.0 0.6 %copy-done.7 = s32[64]{0:T(128)S(1)} copy-done((s32[64]{0:T(128)S(1)}, s32[64]{0:T(128)}, u32[]{:S(2)}) %copy-start.7) | copy-done | bytes 280
  0.7 0.1 pad_dynamic-slice_fusion
  0.7 0.0 copy-start.6
  0.7 0.0 copy-start.4
  0.8 0.7 %copy-done.6 = f32[4,15]{1,0:T(4,128)S(1)} copy-done((f32[4,15]{1,0:T(4,128)S(1)}, f32[4,15]{1,0:T(4,128)}, u32[]{:S(2)}) %copy-start.6) | copy-done | bytes 264
  1.4 0.2 select_reduce_fusion.4
  1.6 0.1 copy.12
  1.7 0.0 copy-done.4
  1.7 0.0 copy-start.5
  1.7 0.1 copy.11
  1.8 0.6 %copy-done.5 = f32[16,15]{1,0:T(8,128)S(1)} copy-done((f32[16,15]{1,0:T(8,128)S(1)}, f32[16,15]{1,0:T(8,128)}, u32[]{:S(2)}) %copy-start.5) | copy-done | bytes 984
  2.4 0.1 copy.13
  2.5 0.0 copy-start.1
  2.5 0.1 select_reduce_fusion.2
  2.6 0.0 copy-start
  2.6 0.1 slice.4
  2.7 0.1 copy.14.lonc
  2.8 0.1 select_reduce_fusion
  2.9 0.1 broadcast_multiply_fusion.1
  3.0 0.2 mul.55
  3.2 0.1 broadcast_multiply_fusion
  3.3 0.2 mul.59
  3.5 0.2 copy-done.1
  3.7 0.4 copy-done
  4.0 0.0 copy-start.2
  4.0 1.0 %copy-done.2 = s32[4,32,1024]{2,1,0:T(8,128)S(1)} copy-done((s32[4,32,1024]{2,1,0:T(8,128)S(1)}, s32[4,32,1024]{2,1,0:T(8,128)}, u32[]{:S(2)}) %copy-start.2) | copy-done | bytes 524312
  5.1 0.0 copy-start.3
  5.1 1.0 %copy-done.3 = f32[4,32,1024]{2,1,0:T(8,128)S(1)} copy-done((f32[4,32,1024]{2,1,0:T(8,128)S(1)}, f32[4,32,1024]{2,1,0:T(8,128)}, u32[]{:S(2)}) %copy-start.3) | copy-done | bytes 524312
  6.1 44.0 %shard_map.82 = f32[2,4,32,1024]{3,2,1,0:T(8,128)S(1)} custom-call(f32[2,4,32,1024]{3,2,1,0:T(8,128)S(1)} %copy-done, f32[2,4,32,1024]{3,2,1,0:T(8,128)S(1)} %copy-done.1, s32[4,32,1024]{2,1,0:T(8,128)S(1)} %copy-done.2, f32[4,32,1024]{2,1,0:T(8,128)S(1)} %copy-done.3, f32[2,128,192]{2,1,0:T(8,128)S(1)} %pad_maximum_fusion.g_ref, f32[48,15]{1,0:T(8,128)S(1)} %copy.14.lonc), custom_call_target="tpu_custom_call" | custom-call | tf_op jit(solution)/shard_map/pallas_call | solution.py:404
  50.1 1.0 %copy.16 = f32[2,4,32,1024]{3,2,1,0:T(8,128)} copy(f32[2,4,32,1024]{3,2,1,0:T(8,128)S(1)} %shard_map.82) | data formatting | bytes 2097152
  (7 shorter events, 0.1 us)
Async XLA Ops:
  0.0 0.7 %copy-start.7 = (s32[64]{0:T(128)S(1)}, s32[64]{0:T(128)}, u32[]{:S(2)}) copy-start(s32[64]{0:T(128)} %param.12) | copy-start | bytes 772
  0.7 0.7 %copy-start.6 = (f32[4,15]{1,0:T(4,128)S(1)}, f32[4,15]{1,0:T(4,128)}, u32[]{:S(2)}) copy-start(f32[4,15]{1,0:T(4,128)} %param.15) | copy-start | bytes 724
  0.7 0.9 %copy-start.4 = (f32[16,15]{1,0:T(8,128)S(1)}, f32[16,15]{1,0:T(8,128)}, u32[]{:S(2)}) copy-start(f32[16,15]{1,0:T(8,128)} %param.13) | copy-start | bytes 2884
  1.7 0.7 %copy-start.5 = (f32[16,15]{1,0:T(8,128)S(1)}, f32[16,15]{1,0:T(8,128)}, u32[]{:S(2)}) copy-start(f32[16,15]{1,0:T(8,128)} %param.14) | copy-start | bytes 2884
  2.5 1.2 %copy-start.1 = (f32[2,4,32,1024]{3,2,1,0:T(8,128)S(1)}, f32[2,4,32,1024]{3,2,1,0:T(8,128)}, u32[]{:S(2)}) copy-start(f32[2,4,32,1024]{3,2,1,0:T(8,128)} %pert.1) | copy-start | bytes 3145732
  2.6 1.4 %copy-start = (f32[2,4,32,1024]{3,2,1,0:T(8,128)S(1)}, f32[2,4,32,1024]{3,2,1,0:T(8,128)}, u32[]{:S(2)}) copy-start(f32[2,4,32,1024]{3,2,1,0:T(8,128)} %ctrl.1) | copy-start | bytes 3145732
  4.0 1.0 %copy-start.2 = (s32[4,32,1024]{2,1,0:T(8,128)S(1)}, s32[4,32,1024]{2,1,0:T(8,128)}, u32[]{:S(2)}) copy-start(s32[4,32,1024]{2,1,0:T(8,128)} %mask.1) | copy-start | bytes 1572868
  5.1 1.0 %copy-start.3 = (f32[4,32,1024]{2,1,0:T(8,128)S(1)}, f32[4,32,1024]{2,1,0:T(8,128)}, u32[]{:S(2)}) copy-start(f32[4,32,1024]{2,1,0:T(8,128)} %wgt.1) | copy-start | bytes 1572868

commit v2 on v1

--- a/solution.py
+++ b/solution.py
@@ -11,39 +11,55 @@
 SUB = 8
 
 
-def by_offset(coefs, offset):
-    taps = jnp.arange(coefs.shape[-1], dtype=jnp.int32)
-    hit = offset[..., None] == taps
-    return jnp.sum(jnp.where(hit, coefs, 0.0), axis=-1)
-
-
-def lookup(classes, valid, table):
-    rows = jnp.arange(table.shape[0], dtype=jnp.int32)
-    hit = (classes[:, None] == rows[None, :]) & valid[:, None]
-    return jnp.sum(jnp.where(hit[:, :, None], table[None], 0.0), axis=1)
-
-
-def matrices(lat_class, lat_table, lon_table, lev_table, rows, levels):
-    taps = lat_table.shape[1]
+PRECISE = lax.Precision.HIGHEST
+
+
+def contract(a, b, precision=None):
+    return lax.dot_general(
+        a, b, (((0,), (0,)), ((), ())), precision=precision, preferred_element_type=jnp.float32
+    )
+
+
+def matrices(lat, classes, lat_tab, lon_tab, lev, G, B, levels, rows):
+    n_classes, taps = lat_tab.shape
+    n_lat = classes.shape[1]
     h = taps // 2
     ext = rows + 2 * SUB
-    first = lax.axis_index("lat") * rows
-    classes = lax.dynamic_slice_in_dim(jnp.pad(lat_class, (SUB, SUB)), first, ext, 0)
-    where = first - SUB + jnp.arange(ext, dtype=jnp.int32)
-    valid = (where >= 0) & (where < lat_class.shape[0])
-    lat_ext = lookup(classes, valid, lat_table)
-    lon_ext = lookup(classes, valid, lon_table)
-    i = jnp.arange(rows, dtype=jnp.int32)[:, None]
-    e = jnp.arange(ext, dtype=jnp.int32)[None, :]
-    ahead = by_offset(lat_ext[SUB : SUB + rows][:, None, :], e - SUB - i + h)
-    ahead = jnp.where(valid[None, :], ahead, 0.0)
-    back = by_offset(lat_ext[None, :, :], i - (e - SUB) + h)
-    l = jnp.arange(levels, dtype=jnp.int32)
-    mix = by_offset(lev_table[:, None, :], l[None, :] - l[:, None] + h)
-    g = mix[:, None, :, None] * ahead[None, :, None, :]
-    gt = mix.T[:, None, :, None] * back[None, :, None, :]
-    both = jnp.stack([g, gt]).reshape(2, levels * rows, levels * ext)
-    return both, lon_ext
+    wide, n_rows = levels * ext, levels * rows
+    start = lat * rows - SUB
+    hit = lax.broadcasted_iota(jnp.int32, (n_classes, n_lat), 0) == classes[...]
+    block = lax.broadcasted_iota(jnp.int32, (1, wide), 1)
+    for l in range(1, levels):
+        block = jnp.where(lax.broadcasted_iota(jnp.int32, (1, wide), 1) >= l * ext, block - ext, block)
+    level = lax.broadcasted_iota(jnp.int32, (1, wide), 1)
+    pick = lax.broadcasted_iota(jnp.int32, (n_lat, wide), 0) == block + start
+    one = lambda x: jnp.where(x, 1.0, 0.0)
+    onehot = jnp.dot(one(hit), one(pick), preferred_element_type=jnp.float32)
+    onehot_ext = onehot[:, :ext]
+    lat_rows = contract(onehot_ext, lat_tab[...], PRECISE)
+    lat_lanes = contract(lat_tab[...], onehot, PRECISE)
+    lon_rows = contract(onehot_ext, lon_tab[...], PRECISE)
+    for t in range(taps):
+        B[t] = jnp.broadcast_to(lon_rows[:, t : t + 1], (ext, LANES))
+    i = lax.broadcasted_iota(jnp.int32, (rows, wide), 0)
+    e = block - SUB
+    inside = (e + lat * rows >= 0) & (e + lat * rows < n_lat)
+    ahead = jnp.zeros((rows, wide), jnp.float32)
+    back = jnp.zeros((rows, wide), jnp.float32)
+    for t in range(taps):
+        ahead = jnp.where((e - i + h == t) & inside, lat_rows[SUB : SUB + rows, t : t + 1], ahead)
+        back = jnp.where(i - e + h == t, lat_lanes[t : t + 1, :], back)
+    for l in range(levels):
+        over, under = jnp.zeros((1, wide), jnp.float32), jnp.zeros((1, wide), jnp.float32)
+        for p in range(levels):
+            there = (level >= p * ext) & (level < (p + 1) * ext)
+            if abs(p - l) <= h:
+                over = jnp.where(there, lev[l, p - l + h], over)
+                under = jnp.where(there, lev[p, l - p + h], under)
+        for a, m in ((0, ahead * over), (1, back * under)):
+            hi, lo = split(m)
+            G[a, l * rows : (l + 1) * rows] = hi
+            G[a, n_rows + l * rows : n_rows + (l + 1) * rows] = lo
 
 
 def split(x):
@@ -52,7 +68,7 @@
 
 
 def kernel(
-    dims, ctrl, pert, mask, wgt, g_ref, lonc, out,
+    dims, ctrl, pert, mask, wgt, classes, lat_tab, lon_tab, lev, out,
     X, Q, Wt, Mk, S, SR, CR, U, Y, D, V, F, R1, R2, WH, B, GS,
     loc, ysend, yrecv, xsend, xrecv, csend, crecv, s1, r1, s2, r2, s3, r3, s4, r4, s5, r5,
 ):
@@ -123,13 +139,8 @@
             for copy in row_copies(side, there):
                 copy.start()
 
-    for t in range(taps):
-        B[t] = jnp.broadcast_to(lonc[:, t : t + 1], (ext, LANES))
+    matrices(lat, classes, lat_tab, lon_tab, lev, GS, B, levels, rows)
     n_rows = levels * rows
-    for a in range(2):
-        hi, lo = split(g_ref[a])
-        GS[a, 0:n_rows] = hi
-        GS[a, n_rows : 2 * n_rows] = lo
 
     lane = lax.broadcasted_iota(jnp.int32, (SUB, LANES), 1)
     windows = [(16, 32 * m) for m in range(members)]
@@ -394,7 +405,6 @@
         nt = -(-(levels * rt_n * nb) // n_mem) * n_mem
         chips = n_mem // 2
         shard = nt // n_mem
-        both, lon_ext = matrices(lat_class, lat_table, lon_table, lev_table, rows, levels)
         dims = (n_mem, n_lat, n_lon, members, levels, rows, cols, taps, nt)
         f32 = jnp.float32
         dma = pltpu.SemaphoreType.DMA
@@ -404,7 +414,7 @@
         return pl.pallas_call(
             functools.partial(kernel, dims),
             out_shape=jax.ShapeDtypeStruct(controls.shape, f32),
-            in_specs=[hbm] * 4 + [vmem] * 2,
+            in_specs=[hbm] * 4 + [vmem] * 3 + [pl.BlockSpec(memory_space=pltpu.SMEM)],
             out_specs=vmem,
             scratch_shapes=[
                 pltpu.VMEM((members, levels, ext, width), f32),
@@ -425,9 +435,9 @@
                 dma((chips,)), dma((chips,)), dma((2,)), dma((2,)),
             ],
             compiler_params=pltpu.CompilerParams(
-                collective_id=0, has_side_effects=True, vmem_limit_bytes=48 * 1024 * 1024
+                collective_id=0, has_side_effects=True, vmem_limit_bytes=62 * 1024 * 1024
             ),
-        )(controls, perturbations, obs_mask, obs_weight, both, lon_ext)
+        )(controls, perturbations, obs_mask, obs_weight, lat_class[None], lat_table, lon_table, lev_table)
 
     return jax.shard_map(
         per_device,

time: 51.4 us -> 48.4 us (0.942)
  local copies, waits for them, and re-layouts: 6.32 us -> 2.31 us
  Pallas kernels: 44 us -> 45.8 us
  other arithmetic: 0.7 us -> 0 us
    unnamed x19 -> x1, local copies, waits for them, and re-layouts: 5.66 us -> 2.31 us
    pallas_call x1, Pallas kernels: 44 us -> 45.8 us  [per_device(): pl.pallas_call(functools.partial(kernel, dims), out_shape=jax.ShapeDtypeS...]
where the time goes in v2:
time: 48.4 us; the launch traced here: 48.2 us
  Pallas kernels  45.8 us (95%)
  local copies, waits for them, and re-layouts  2.31 us (5%)
    pallas_call x1, Pallas kernels, per_device(): pl.pallas_call(functools.partial(kernel, dims), out_shape=jax.ShapeDtypeS...  45.8 us
    unnamed x1, local copies, waits for them, and re-layouts  2.31 us

profile of v2, /device:TPU:0, one launch (start us, length us, event | category | flops | bytes accessed | tf_op | source)
XLA Modules:
  0.0 48.2 jit_solution(4660484544716227921)
XLA Ops:
  0.0 45.8 %shard_map.82 = f32[2,4,32,1024]{3,2,1,0:T(8,128)} custom-call(f32[2,4,32,1024]{3,2,1,0:T(8,128)} %ctrl.1, f32[2,4,32,1024]{3,2,1,0:T(8,128)} %pert.1, s32[4,32,1024]{2,1,0:T(8,128)} %mask.1, f32[4,32,1024]{2,1,0:T(8,128)} %wgt.1, s32[1,64]{1,0:T(1,128)} %bitcast.1, f32[16,15]{1,0:T(8,128)} %lat_tab.1, f32[16,15]{1,0:T(8,128)} %lon_tab.1, f32[4,15]{1,0:T(4,128)} %lev.1), custom_call_target="tpu_custom_call" | custom-call | tf_op jit(solution)/shard_map/pallas_call | solution.py:414
  45.8 2.3 %copy.10 = f32[2,4,32,1024]{3,2,1,0:T(8,128)} copy(f32[2,4,32,1024]{3,2,1,0:T(8,128)} %shard_map.82) | data formatting | bytes 2097152

commit v3 on v2

--- a/solution.py
+++ b/solution.py
@@ -82,6 +82,11 @@
     half = nt // 2
     shard = half // chips
     edge = levels * nb
+    n_half = levels * rt_n // 2
+
+    def tile_of(idx):
+        return idx // n_half * half + lax.rem(idx, n_half) * nb
+
     mem, lat, lon = lax.axis_index("mem"), lax.axis_index("lat"), lax.axis_index("lon")
     z, c = mem // 2, lax.rem(mem, 2)
     sib = mem + 1 - 2 * c
@@ -136,11 +141,7 @@
     for there, exists, side in lat_to:
         @pl.when(exists)
         def _():
-            for copy in row_copies(side, there):
-                copy.start()
-
-    matrices(lat, classes, lat_tab, lon_tab, lev, GS, B, levels, rows)
-    n_rows = levels * rows
+            row_copies(side, there)[0].start()
 
     lane = lax.broadcasted_iota(jnp.int32, (SUB, LANES), 1)
     windows = [(16, 32 * m) for m in range(members)]
@@ -185,6 +186,9 @@
             for copy in corner_copies(side, there):
                 copy.start()
 
+    matrices(lat, classes, lat_tab, lon_tab, lev, GS, B, levels, rows)
+    n_rows = levels * rows
+
     for side, there, exists in ((0, lat - 1, lat > 0), (1, lat + 1, lat < n_lat - 1)):
         its = pl.ds(rows + SUB if side else 0, SUB)
 
@@ -200,7 +204,7 @@
         r = pl.ds(pl.multiple_of(rt * SUB, SUB), SUB)
         for b in range(nb - 1):
             at = pl.ds(b * LANES, LANES)
-            V[idx * nb + b] = Wt[l, r, at] * Mk[l, r, at].astype(jnp.float32)
+            V[tile_of(idx) + b] = Wt[l, r, at] * Mk[l, r, at].astype(jnp.float32)
         return carry
 
     lax.fori_loop(0, levels * rt_n, weigh, 0)
@@ -229,7 +233,7 @@
             elif w < 2 * members:
                 Q[w - members, l, pl.ds(r + SUB, SUB), strip] = value
             else:
-                V[idx * nb + nb - 1] = value
+                V[tile_of(idx) + nb - 1] = value
         return carry
 
     lax.fori_loop(0, levels * rt_n, spread_strip, 0)
@@ -238,6 +242,7 @@
         @pl.when(exists)
         def _():
             row_copies(side, there)[0].wait_send()
+            row_copies(side, there)[1].start()
             for copy in corner_copies(side, there):
                 copy.wait_send()
     for side, there, exists in ((0, lat - 1, lat > 0), (1, lat + 1, lat < n_lat - 1)):
@@ -286,28 +291,26 @@
             term = Q[m, l, pl.ds(r + SUB, SUB)] * along(U[m, l, pl.ds(r, SUB)], rt + 1, True)
             total = term if total is None else total + term
         for b in range(nb):
-            D[idx * nb + b] = total[:, b * LANES : (b + 1) * LANES]
+            D[tile_of(idx) + b] = total[:, b * LANES : (b + 1) * LANES]
         return carry
 
-    lax.fori_loop(0, levels * rt_n, forward, 0)
-    for i in range(rt_n * edge, nt):
-        D[i] = jnp.zeros((SUB, LANES), jnp.float32)
-        V[i] = jnp.zeros((SUB, LANES), jnp.float32)
+    for g in range(2):
+        for i in range(n_half * nb, half):
+            D[g * half + i] = jnp.zeros((SUB, LANES), jnp.float32)
+            V[g * half + i] = jnp.zeros((SUB, LANES), jnp.float32)
 
     base = c * half
+    other = (1 - c) * n_half
+    lax.fori_loop(other, other + n_half, forward, 0)
     pair = remote(D.at[pl.ds((1 - c) * half, half)], R1, s1, r1, mem=sib)
     pair.start()
+    lax.fori_loop(c * n_half, c * n_half + n_half, forward, 0)
     pair.wait_recv()
     to_owner = []
     for k in range(1, chips):
         tz = lax.rem(z + k, chips)
         at = tz * shard
-
-        def add(i, carry, at=at):
-            D[base + at + i] += R1[at + i]
-            return carry
-
-        lax.fori_loop(0, shard, add, 0)
+        D[pl.ds(base + at, shard)] += R1[pl.ds(at, shard)]
         copy = remote(D.at[pl.ds(base + at, shard)], R2.at[k - 1], s2.at[k - 1], r2.at[k - 1], mem=tz * 2 + c)
         copy.start()
         to_owner.append(copy)
@@ -316,14 +319,10 @@
 
     own = z * shard
 
-    def finish(i, carry):
-        total = D[base + own + i] + R1[own + i]
-        for k in range(1, chips):
-            total += R2[k - 1, i]
-        F[base + own + i] = total * V[base + own + i]
-        return carry
-
-    lax.fori_loop(0, shard, finish, 0)
+    total = D[pl.ds(base + own, shard)] + R1[pl.ds(own, shard)]
+    for k in range(1, chips):
+        total += R2[k - 1]
+    F[pl.ds(base + own, shard)] = total * V[pl.ds(base + own, shard)]
 
     mine = F.at[pl.ds(base + own, shard)]
     back = [
@@ -343,7 +342,7 @@
         copy.wait_recv()
 
     def edge_copy(side, there):
-        at = 0 if side else (rt_n - 1) * edge
+        at = 0 if side else half + (rt_n // 2 - 1) * edge
         return remote(F.at[pl.ds(at, edge)], WH.at[side], s5.at[side], r5.at[side], lat=there)
 
     for there, exists, side in lat_to:
@@ -359,7 +358,7 @@
     def backward(idx, carry):
         rt, l = idx // levels, lax.rem(idx, levels)
         r = pl.multiple_of(rt * SUB + SUB, SUB)
-        backward_tile(l, r, rt + 1, lambda b: F[idx * nb + b])
+        backward_tile(l, r, rt + 1, lambda b: F[tile_of(idx) + b])
         return carry
 
     lax.fori_loop(0, levels * rt_n, backward, 0)
@@ -402,7 +401,7 @@
         taps = lat_table.shape[1]
         nb = cols // LANES + 1
         width, ext, rt_n = nb * LANES, rows + 2 * SUB, rows // SUB
-        nt = -(-(levels * rt_n * nb) // n_mem) * n_mem
+        nt = 2 * (-(-(levels * rt_n // 2 * nb) // (n_mem // 2)) * (n_mem // 2))
         chips = n_mem // 2
         shard = nt // n_mem
         dims = (n_mem, n_lat, n_lon, members, levels, rows, cols, taps, nt)

time: 48.4 us -> 46.2 us (0.955)
  the two profiles are of different devices: /device:TPU:0 before, /device:TPU:1 now
where the time goes in v3:
time: 46.2 us; the launch traced here: 46 us
  Pallas kernels  43.7 us (95%)
  local copies, waits for them, and re-layouts  2.31 us (5%)
    pallas_call x1, Pallas kernels, per_device(): pl.pallas_call(functools.partial(kernel, dims), out_shape=jax.ShapeDtypeS...  43.7 us
    unnamed x1, local copies, waits for them, and re-layouts  2.31 us

profile of v3, /device:TPU:1, one launch (start us, length us, event | category | flops | bytes accessed | tf_op | source)
XLA Modules:
  0.0 46.0 jit_solution(3037717401898119272)
XLA Ops:
  0.0 43.7 %shard_map.82 = f32[2,4,32,1024]{3,2,1,0:T(8,128)} custom-call(f32[2,4,32,1024]{3,2,1,0:T(8,128)} %ctrl.1, f32[2,4,32,1024]{3,2,1,0:T(8,128)} %pert.1, s32[4,32,1024]{2,1,0:T(8,128)} %mask.1, f32[4,32,1024]{2,1,0:T(8,128)} %wgt.1, s32[1,64]{1,0:T(1,128)} %bitcast.1, f32[16,15]{1,0:T(8,128)} %lat_tab.1, f32[16,15]{1,0:T(8,128)} %lon_tab.1, f32[4,15]{1,0:T(4,128)} %lev.1), custom_call_target="tpu_custom_call" | custom-call | tf_op jit(solution)/shard_map/pallas_call | solution.py:413
  43.7 2.3 %copy.10 = f32[2,4,32,1024]{3,2,1,0:T(8,128)} copy(f32[2,4,32,1024]{3,2,1,0:T(8,128)} %shard_map.82) | data formatting | bytes 2097152

commit v4 on v3

--- a/solution.py
+++ b/solution.py
@@ -117,11 +117,12 @@
         @pl.when(exists)
         def _():
             greet(lat=there)
+            greet(lat=there, mem=sib)
             for x in lon_to:
                 greet(lat=there, lon=x)
     peers = chips + len(lon_to)
     for _, exists, _ in lat_to:
-        peers += jnp.where(exists, 1 + len(lon_to), 0)
+        peers += jnp.where(exists, 2 + len(lon_to), 0)
     pl.semaphore_wait(barrier, peers)
 
     def remote(src, dst, send, recv, **where):
@@ -338,17 +339,19 @@
         copy = remote(got, got, s4.at[k], r4.at[k], mem=sib)
         copy.start()
         passed.append(copy)
-    for copy in passed:
-        copy.wait_recv()
-
-    def edge_copy(side, there):
+
+    def edge_copies(side, there):
         at = 0 if side else half + (rt_n // 2 - 1) * edge
-        return remote(F.at[pl.ds(at, edge)], WH.at[side], s5.at[side], r5.at[side], lat=there)
+        return [
+            remote(F.at[pl.ds(at, edge)], WH.at[side], s5.at[side, a], r5.at[side], lat=there, mem=m)
+            for a, m in enumerate((mem, sib))
+        ]
 
     for there, exists, side in lat_to:
-        @pl.when(exists)
-        def _():
-            edge_copy(side, there).start()
+        @pl.when(exists & (c == 1 - side))
+        def _():
+            for copy in edge_copies(side, there):
+                copy.start()
 
     def backward_tile(l, r, tile, read):
         w = jnp.concatenate([read(b) for b in range(nb)], axis=1)
@@ -361,7 +364,10 @@
         backward_tile(l, r, rt + 1, lambda b: F[tile_of(idx) + b])
         return carry
 
-    lax.fori_loop(0, levels * rt_n, backward, 0)
+    lax.fori_loop(c * n_half, c * n_half + n_half, backward, 0)
+    for copy in passed:
+        copy.wait_recv()
+    lax.fori_loop(other, other + n_half, backward, 0)
 
     for side, there, exists in ((0, lat - 1, lat > 0), (1, lat + 1, lat < n_lat - 1)):
         tile = rt_n + 1 if side else 0
@@ -369,7 +375,7 @@
         @pl.when(exists)
         def _():
             row_copies(side, there)[1].wait_recv()
-            edge_copy(side, there).wait_recv()
+            edge_copies(side, there)[0].wait_recv()
 
             def halo(l, carry):
                 backward_tile(l, tile * SUB, tile, lambda b: WH[side, l * nb + b])
@@ -390,7 +396,11 @@
         @pl.when(exists)
         def _():
             row_copies(side, there)[1].wait_send()
-            edge_copy(side, there).wait_send()
+
+        @pl.when(exists & (c == 1 - side))
+        def _():
+            for copy in edge_copies(side, there):
+                copy.wait_send()
 
 
 def solution(mesh):
@@ -431,7 +441,7 @@
                 pltpu.VMEM((2, 2 * levels * rows, levels * ext), jnp.bfloat16),
                 dma((4,)), dma((2, 2)), dma((2, 2)), dma((sides,)), dma((sides,)), dma((2, sides)), dma((2, sides)),
                 dma(()), dma(()), dma((chips,)), dma((chips,)), dma((chips,)), dma((chips,)),
-                dma((chips,)), dma((chips,)), dma((2,)), dma((2,)),
+                dma((chips,)), dma((chips,)), dma((2, 2)), dma((2,)),
             ],
             compiler_params=pltpu.CompilerParams(
                 collective_id=0, has_side_effects=True, vmem_limit_bytes=62 * 1024 * 1024

time: 46.2 us -> 45.2 us (0.978)
  the two profiles are of different devices: /device:TPU:1 before, /device:TPU:0 now
where the time goes in v4:
time: 45.2 us; the launch traced here: 45 us
  Pallas kernels  42.7 us (94%)
  local copies, waits for them, and re-layouts  2.31 us (5%)
    pallas_call x1, Pallas kernels, per_device(): pl.pallas_call(functools.partial(kernel, dims), out_shape=jax.ShapeDtypeS...  42.7 us
    unnamed x1, local copies, waits for them, and re-layouts  2.31 us

profile of v4, /device:TPU:0, one launch (start us, length us, event | category | flops | bytes accessed | tf_op | source)
XLA Modules:
  0.0 45.0 jit_solution(4802566116565407429)
XLA Ops:
  0.0 42.7 %shard_map.82 = f32[2,4,32,1024]{3,2,1,0:T(8,128)} custom-call(f32[2,4,32,1024]{3,2,1,0:T(8,128)} %ctrl.1, f32[2,4,32,1024]{3,2,1,0:T(8,128)} %pert.1, s32[4,32,1024]{2,1,0:T(8,128)} %mask.1, f32[4,32,1024]{2,1,0:T(8,128)} %wgt.1, s32[1,64]{1,0:T(1,128)} %bitcast.1, f32[16,15]{1,0:T(8,128)} %lat_tab.1, f32[16,15]{1,0:T(8,128)} %lon_tab.1, f32[4,15]{1,0:T(4,128)} %lev.1), custom_call_target="tpu_custom_call" | custom-call | tf_op jit(solution)/shard_map/pallas_call | solution.py:423
  42.7 2.3 %copy.10 = f32[2,4,32,1024]{3,2,1,0:T(8,128)} copy(f32[2,4,32,1024]{3,2,1,0:T(8,128)} %shard_map.82) | data formatting | bytes 2097152

commit v5 on v4

--- a/solution.py
+++ b/solution.py
@@ -79,13 +79,13 @@
     rt_n = rows // SUB
     ext = rows + 2 * SUB
     chips = n_mem // 2
-    half = nt // 2
-    shard = half // chips
+    quarter = nt // 4
+    shard = quarter // chips
     edge = levels * nb
-    n_half = levels * rt_n // 2
+    n_quarter = levels * rt_n // 4
 
     def tile_of(idx):
-        return idx // n_half * half + lax.rem(idx, n_half) * nb
+        return idx // n_quarter * quarter + lax.rem(idx, n_quarter) * nb
 
     mem, lat, lon = lax.axis_index("mem"), lax.axis_index("lat"), lax.axis_index("lon")
     z, c = mem // 2, lax.rem(mem, 2)
@@ -120,6 +120,9 @@
             greet(lat=there, mem=sib)
             for x in lon_to:
                 greet(lat=there, lon=x)
+    matrices(lat, classes, lat_tab, lon_tab, lev, GS, B, levels, rows)
+    n_rows = levels * rows
+
     peers = chips + len(lon_to)
     for _, exists, _ in lat_to:
         peers += jnp.where(exists, 2 + len(lon_to), 0)
@@ -187,9 +190,6 @@
             for copy in corner_copies(side, there):
                 copy.start()
 
-    matrices(lat, classes, lat_tab, lon_tab, lev, GS, B, levels, rows)
-    n_rows = levels * rows
-
     for side, there, exists in ((0, lat - 1, lat > 0), (1, lat + 1, lat < n_lat - 1)):
         its = pl.ds(rows + SUB if side else 0, SUB)
 
@@ -295,63 +295,59 @@
             D[tile_of(idx) + b] = total[:, b * LANES : (b + 1) * LANES]
         return carry
 
-    for g in range(2):
-        for i in range(n_half * nb, half):
-            D[g * half + i] = jnp.zeros((SUB, LANES), jnp.float32)
-            V[g * half + i] = jnp.zeros((SUB, LANES), jnp.float32)
-
-    base = c * half
-    other = (1 - c) * n_half
-    lax.fori_loop(other, other + n_half, forward, 0)
-    pair = remote(D.at[pl.ds((1 - c) * half, half)], R1, s1, r1, mem=sib)
-    pair.start()
-    lax.fori_loop(c * n_half, c * n_half + n_half, forward, 0)
-    pair.wait_recv()
-    to_owner = []
-    for k in range(1, chips):
-        tz = lax.rem(z + k, chips)
-        at = tz * shard
-        D[pl.ds(base + at, shard)] += R1[pl.ds(at, shard)]
-        copy = remote(D.at[pl.ds(base + at, shard)], R2.at[k - 1], s2.at[k - 1], r2.at[k - 1], mem=tz * 2 + c)
+    for g in range(4):
+        for i in range(n_quarter * nb, quarter):
+            D[g * quarter + i] = jnp.zeros((SUB, LANES), jnp.float32)
+            V[g * quarter + i] = jnp.zeros((SUB, LANES), jnp.float32)
+
+    own_q = [step + c * (3 - 2 * step) for step in range(2)]
+    sib_q = [step + (1 - c) * (3 - 2 * step) for step in range(2)]
+
+    def over(q, body):
+        lax.fori_loop(q * n_quarter, q * n_quarter + n_quarter, body, 0)
+
+    def part(q, chip):
+        return pl.ds(q * quarter + chip * shard, shard)
+
+    pairs, to_owner, back, passed = [], [[], []], [[], []], [[], []]
+    for step in range(2):
+        over(sib_q[step], forward)
+        pair = remote(D.at[pl.ds(sib_q[step] * quarter, quarter)], R1.at[step], s1.at[step], r1.at[step], mem=sib)
+        pair.start()
+        pairs.append(pair)
+    for step in range(2):
+        over(own_q[step], forward)
+        pairs[step].wait_recv()
+        for k in range(1, chips):
+            tz = lax.rem(z + k, chips)
+            here = part(own_q[step], tz)
+            D[here] += R1[step, pl.ds(tz * shard, shard)]
+            copy = remote(D.at[here], R2.at[step, k - 1], s2.at[step, k - 1], r2.at[step, k - 1], mem=tz * 2 + c)
+            copy.start()
+            to_owner[step].append(copy)
+    for step in range(2):
+        for copy in to_owner[step]:
+            copy.wait_recv()
+        here = part(own_q[step], z)
+        total = D[here] + R1[step, pl.ds(z * shard, shard)]
+        for k in range(1, chips):
+            total += R2[step, k - 1]
+        F[here] = total * V[here]
+        mine = F.at[here]
+        for k in range(1, chips):
+            copy = remote(mine, mine, s3.at[step, k - 1], r3.at[step, k - 1], mem=lax.rem(z + k, chips) * 2 + c)
+            copy.start()
+            back[step].append(copy)
+        copy = remote(mine, mine, s4.at[step, 0], r4.at[step, 0], mem=sib)
         copy.start()
-        to_owner.append(copy)
-    for copy in to_owner:
-        copy.wait_recv()
-
-    own = z * shard
-
-    total = D[pl.ds(base + own, shard)] + R1[pl.ds(own, shard)]
-    for k in range(1, chips):
-        total += R2[k - 1]
-    F[pl.ds(base + own, shard)] = total * V[pl.ds(base + own, shard)]
-
-    mine = F.at[pl.ds(base + own, shard)]
-    back = [
-        remote(mine, mine, s3.at[k - 1], r3.at[k - 1], mem=lax.rem(z + k, chips) * 2 + c)
-        for k in range(1, chips)
-    ]
-    passed = [remote(mine, mine, s4.at[0], r4.at[0], mem=sib)]
-    for copy in back + passed:
-        copy.start()
-    for k in range(1, chips):
-        back[k - 1].wait_recv()
-        got = F.at[pl.ds(base + lax.rem(z - k + chips, chips) * shard, shard)]
-        copy = remote(got, got, s4.at[k], r4.at[k], mem=sib)
-        copy.start()
-        passed.append(copy)
+        passed[step].append(copy)
 
     def edge_copies(side, there):
-        at = 0 if side else half + (rt_n // 2 - 1) * edge
+        at = 0 if side else 3 * quarter + n_quarter * nb - edge
         return [
             remote(F.at[pl.ds(at, edge)], WH.at[side], s5.at[side, a], r5.at[side], lat=there, mem=m)
             for a, m in enumerate((mem, sib))
         ]
-
-    for there, exists, side in lat_to:
-        @pl.when(exists & (c == 1 - side))
-        def _():
-            for copy in edge_copies(side, there):
-                copy.start()
 
     def backward_tile(l, r, tile, read):
         w = jnp.concatenate([read(b) for b in range(nb)], axis=1)
@@ -364,10 +360,24 @@
         backward_tile(l, r, rt + 1, lambda b: F[tile_of(idx) + b])
         return carry
 
-    lax.fori_loop(c * n_half, c * n_half + n_half, backward, 0)
-    for copy in passed:
-        copy.wait_recv()
-    lax.fori_loop(other, other + n_half, backward, 0)
+    for step in range(2):
+        for k in range(1, chips):
+            back[step][k - 1].wait_recv()
+            got = F.at[part(own_q[step], lax.rem(z - k + chips, chips))]
+            copy = remote(got, got, s4.at[step, k], r4.at[step, k], mem=sib)
+            copy.start()
+            passed[step].append(copy)
+        if step == 0:
+            for there, exists, side in lat_to:
+                @pl.when(exists & (c == 1 - side))
+                def _():
+                    for copy in edge_copies(side, there):
+                        copy.start()
+        over(own_q[step], backward)
+    for step in range(2):
+        for copy in passed[step]:
+            copy.wait_recv()
+        over(sib_q[step], backward)
 
     for side, there, exists in ((0, lat - 1, lat > 0), (1, lat + 1, lat < n_lat - 1)):
         tile = rt_n + 1 if side else 0
@@ -389,8 +399,7 @@
             y = Y[m, :, :, at].reshape(levels * ext, 2 * LANES)
             out[m, :, :, at] = X[m, :, SUB : SUB + rows, at] + product(1, y).reshape(levels, rows, 2 * LANES)
 
-    pair.wait_send()
-    for copy in to_owner + back + passed:
+    for copy in pairs + to_owner[0] + to_owner[1] + back[0] + back[1] + passed[0] + passed[1]:
         copy.wait_send()
     for there, exists, side in lat_to:
         @pl.when(exists)
@@ -411,9 +420,9 @@
         taps = lat_table.shape[1]
         nb = cols // LANES + 1
         width, ext, rt_n = nb * LANES, rows + 2 * SUB, rows // SUB
-        nt = 2 * (-(-(levels * rt_n // 2 * nb) // (n_mem // 2)) * (n_mem // 2))
+        nt = 4 * (-(-(levels * rt_n // 4 * nb) // (n_mem // 2)) * (n_mem // 2))
         chips = n_mem // 2
-        shard = nt // n_mem
+        shard = nt // 4 // chips
         dims = (n_mem, n_lat, n_lon, members, levels, rows, cols, taps, nt)
         f32 = jnp.float32
         dma = pltpu.SemaphoreType.DMA
@@ -436,12 +445,11 @@
                 pltpu.VMEM((members, levels, rows, width), f32),
                 pltpu.VMEM((members, levels, ext, cols), f32),
                 tiles(nt), tiles(nt), tiles(nt),
-                tiles(nt // 2), tiles(max(chips - 1, 1), shard), tiles(2, levels * nb),
+                tiles(2, nt // 4), tiles(2, max(chips - 1, 1), shard), tiles(2, levels * nb),
                 pltpu.VMEM((taps, ext, LANES), f32),
                 pltpu.VMEM((2, 2 * levels * rows, levels * ext), jnp.bfloat16),
                 dma((4,)), dma((2, 2)), dma((2, 2)), dma((sides,)), dma((sides,)), dma((2, sides)), dma((2, sides)),
-                dma(()), dma(()), dma((chips,)), dma((chips,)), dma((chips,)), dma((chips,)),
-                dma((chips,)), dma((chips,)), dma((2, 2)), dma((2,)),
+                dma((2,)), dma((2,)), *[dma((2, chips))] * 6, dma((2, 2)), dma((2,)),
             ],
             compiler_params=pltpu.CompilerParams(
                 collective_id=0, has_side_effects=True, vmem_limit_bytes=62 * 1024 * 1024

time: 45.2 us -> 43.9 us (0.971)
  Pallas kernels: 42.7 us -> 41.4 us
    pallas_call x1, Pallas kernels: 42.7 us -> 41.4 us  [per_device(): pl.pallas_call(functools.partial(kernel, dims), out_shape=jax.ShapeDtypeS...]
where the time goes in v5:
time: 43.9 us; the launch traced here: 43.8 us
  Pallas kernels  41.4 us (94%)
  local copies, waits for them, and re-layouts  2.31 us (5%)
    pallas_call x1, Pallas kernels, per_device(): pl.pallas_call(functools.partial(kernel, dims), out_shape=jax.ShapeDtypeS...  41.4 us
    unnamed x1, local copies, waits for them, and re-layouts  2.31 us

profile of v5, /device:TPU:0, one launch (start us, length us, event | category | flops | bytes accessed | tf_op | source)
XLA Modules:
  0.0 43.8 jit_solution(2834819269385967377)
XLA Ops:
  0.0 41.4 %shard_map.82 = f32[2,4,32,1024]{3,2,1,0:T(8,128)} custom-call(f32[2,4,32,1024]{3,2,1,0:T(8,128)} %ctrl.1, f32[2,4,32,1024]{3,2,1,0:T(8,128)} %pert.1, s32[4,32,1024]{2,1,0:T(8,128)} %mask.1, f32[4,32,1024]{2,1,0:T(8,128)} %wgt.1, s32[1,64]{1,0:T(1,128)} %bitcast.1, f32[16,15]{1,0:T(8,128)} %lat_tab.1, f32[16,15]{1,0:T(8,128)} %lon_tab.1, f32[4,15]{1,0:T(4,128)} %lev.1), custom_call_target="tpu_custom_call" | custom-call | tf_op jit(solution)/shard_map/pallas_call | solution.py:432
  41.4 2.3 %copy.10 = f32[2,4,32,1024]{3,2,1,0:T(8,128)} copy(f32[2,4,32,1024]{3,2,1,0:T(8,128)} %shard_map.82) | data formatting | bytes 2097152

commit v6 on v5

--- a/solution.py
+++ b/solution.py
@@ -123,30 +123,6 @@
     matrices(lat, classes, lat_tab, lon_tab, lev, GS, B, levels, rows)
     n_rows = levels * rows
 
-    peers = chips + len(lon_to)
-    for _, exists, _ in lat_to:
-        peers += jnp.where(exists, 2 + len(lon_to), 0)
-    pl.semaphore_wait(barrier, peers)
-
-    def remote(src, dst, send, recv, **where):
-        return pltpu.make_async_remote_copy(
-            src_ref=src, dst_ref=dst, send_sem=send, recv_sem=recv,
-            device_id=where, device_id_type=pl.DeviceIdType.MESH,
-        )
-
-    def row_copies(side, there):
-        mine = pl.ds(0 if side else rows - SUB, SUB)
-        its = pl.ds(rows + SUB if side else 0, SUB)
-        return [
-            remote(src.at[:, :, mine], dst.at[:, :, its, pl.ds(0, cols)], ysend.at[side, a], yrecv.at[side, a], lat=there)
-            for a, (src, dst) in enumerate(((ctrl, X), (pert, Q)))
-        ]
-
-    for there, exists, side in lat_to:
-        @pl.when(exists)
-        def _():
-            row_copies(side, there)[0].start()
-
     lane = lax.broadcasted_iota(jnp.int32, (SUB, LANES), 1)
     windows = [(16, 32 * m) for m in range(members)]
     centre = 32 * members - 8
@@ -172,6 +148,30 @@
         return carry
 
     lax.fori_loop(0, levels * rt_n, pack, 0)
+
+    peers = chips + len(lon_to)
+    for _, exists, _ in lat_to:
+        peers += jnp.where(exists, 2 + len(lon_to), 0)
+    pl.semaphore_wait(barrier, peers)
+
+    def remote(src, dst, send, recv, **where):
+        return pltpu.make_async_remote_copy(
+            src_ref=src, dst_ref=dst, send_sem=send, recv_sem=recv,
+            device_id=where, device_id_type=pl.DeviceIdType.MESH,
+        )
+
+    def row_copies(side, there):
+        mine = pl.ds(0 if side else rows - SUB, SUB)
+        its = pl.ds(rows + SUB if side else 0, SUB)
+        return [
+            remote(src.at[:, :, mine], dst.at[:, :, its, pl.ds(0, cols)], ysend.at[side, a], yrecv.at[side, a], lat=there)
+            for a, (src, dst) in enumerate(((ctrl, X), (pert, Q)))
+        ]
+
+    for there, exists, side in lat_to:
+        @pl.when(exists)
+        def _():
+            row_copies(side, there)[0].start()
 
     strips = [remote(S, SR.at[a], xsend.at[a], xrecv.at[a], lon=x) for a, x in enumerate(lon_to)]
     for copy in strips:

time: 43.9 us -> 44.1 us (level)
  no operation moved by 1% of the time
where the time goes in v6:
time: 44.1 us; the launch traced here: 43.9 us
  Pallas kernels  41.6 us (94%)
  local copies, waits for them, and re-layouts  2.31 us (5%)
    pallas_call x1, Pallas kernels, per_device(): pl.pallas_call(functools.partial(kernel, dims), out_shape=jax.ShapeDtypeS...  41.6 us
    unnamed x1, local copies, waits for them, and re-layouts  2.31 us

profile of v6, /device:TPU:0, one launch (start us, length us, event | category | flops | bytes accessed | tf_op | source)
XLA Modules:
  0.0 43.9 jit_solution(2940758210086592499)
XLA Ops:
  0.0 41.6 %shard_map.82 = f32[2,4,32,1024]{3,2,1,0:T(8,128)} custom-call(f32[2,4,32,1024]{3,2,1,0:T(8,128)} %ctrl.1, f32[2,4,32,1024]{3,2,1,0:T(8,128)} %pert.1, s32[4,32,1024]{2,1,0:T(8,128)} %mask.1, f32[4,32,1024]{2,1,0:T(8,128)} %wgt.1, s32[1,64]{1,0:T(1,128)} %bitcast.1, f32[16,15]{1,0:T(8,128)} %lat_tab.1, f32[16,15]{1,0:T(8,128)} %lon_tab.1, f32[4,15]{1,0:T(4,128)} %lev.1), custom_call_target="tpu_custom_call" | custom-call | tf_op jit(solution)/shard_map/pallas_call | solution.py:432
  41.6 2.3 %copy.10 = f32[2,4,32,1024]{3,2,1,0:T(8,128)} copy(f32[2,4,32,1024]{3,2,1,0:T(8,128)} %shard_map.82) | data formatting | bytes 2097152
